TPU v7x, 32 devices: a whole 2x2x4 slice. The times are simulated.
32 devices in a mesh: space: 16 (over z, y, x), sens: 2 (over core).
Axes of the slice: x: 2, y: 2, z: 4, core: 2. Of those that a mesh axis runs over, the one named last changes fastest.
Arguments:
- adjoint_end: float32 [16, 64, 64, 128], P('sens', 'space'), may hold values from -6 to 6
- checkpoints: float32 [8, 64, 64, 128], P('sens', 'space'), may hold values from 0.5 to 2
- dispersion: float32 [6, 64, 64, 128], P(None, 'space', 'sens'), as said below
- owner_steps: int32 [3], replicated, may hold values from 0 to 7, as said below
- sensor_cells: int32 [16], P('sens'), may hold values from 0 to 524287
- misfit: float32 [16, 3], P('sens'), may hold values from -6 to 6
- release_cells: int32 [128], replicated, may hold values from 0 to 524287
- release_steps: int32 [128], replicated, may hold values from 0 to 2
Outputs:
- adjoint: float32 [16, 64, 64, 128], P('sens', 'space')
- release_grad: float32 [16, 128], P('sens')
Inputs may be any that keep to these rules, and one draw needn't show every extreme that they name: `owner_steps`: the entries are different stored states; the first and the last stored state are always among them. `sensor_cells`: flat cell indices. `release_cells`: flat cell indices. `dispersion`: zz, yy and xx components are positive.
All inputs are finite; a program needn't handle non-finite values.
Results may differ from a plain program's by a relative error of at most 0.00002.
Values sent between devices are 32-bit elements; how exact they have to be, the bound alone decides.
No kernel may reach another device: no remote copies, remote signals or barrier semaphores. Data moves between devices by JAX's collectives and lax.ppermute only.
A program may use at most 128 MiB of HBM per device.

v0:
```python
import jax
import jax.numpy as jnp
from jax import lax
from jax.sharding import PartitionSpec as P

STEPS = 3
step_dt = 0.12


def extended(block, sides, width):
    for axis, dim in sides:
        count = lax.axis_size(axis)
        forward = [(i, i + 1) for i in range(count - 1)]
        backward = [(target, source) for source, target in forward]
        low = lax.ppermute(
            lax.slice_in_dim(block, block.shape[dim] - width, None, axis=dim), axis, forward
        )
        high = lax.ppermute(lax.slice_in_dim(block, 0, width, axis=dim), axis, backward)
        block = jnp.concatenate([low, block, high], axis=dim)
    return block


def broadcast(array, axis, root):
    mine = lax.axis_index(axis) == root
    return lax.psum(jnp.where(mine, array, jnp.zeros_like(array)), axis)


def retard_scale(conc):
    return step_dt / (1.0 + 0.5 * conc ** (-0.5))


def retard_slope(conc):
    retard = 1.0 + 0.5 * conc ** (-0.5)
    deriv = -0.25 * conc ** (-1.5)
    return -step_dt * deriv / (retard * retard)


def apply_op(field, tensor):
    depth = field.shape[1] - 2
    rows_y = field.shape[2]
    rows_x = field.shape[3]
    padded = jnp.pad(field, ((0, 0), (0, 0), (1, 1), (1, 1)))
    coeffs = jnp.pad(tensor, ((0, 0), (0, 0), (1, 1), (1, 1)))

    def at_shift(arr, shift):
        return arr[
            ...,
            1 + shift[0] : 1 + shift[0] + depth,
            1 + shift[1] : 1 + shift[1] + rows_y,
            1 + shift[2] : 1 + shift[2] + rows_x,
        ]

    units = [(1, 0, 0), (0, 1, 0), (0, 0, 1)]
    centre = (0, 0, 0)
    total = jnp.zeros((field.shape[0], depth, rows_y, rows_x), jnp.float32)
    for axis_id in range(3):
        plus = units[axis_id]
        minus = tuple((-v for v in plus))
        diag = coeffs[axis_id]
        a_plus = 0.5 * (at_shift(diag, centre) + at_shift(diag, plus))
        a_minus = 0.5 * (at_shift(diag, centre) + at_shift(diag, minus))
        total = total + a_plus * (at_shift(padded, plus) - at_shift(padded, centre))
        total = total - a_minus * (at_shift(padded, centre) - at_shift(padded, minus))
    for first, second, comp in ((0, 1, 3), (0, 2, 4), (1, 2, 5)):
        for outer, inner in ((first, second), (second, first)):
            unit_o = units[outer]
            unit_i = units[inner]
            for sign in (1, -1):
                spot = tuple((sign * v for v in unit_o))
                up_spot = tuple((spot[t] + unit_i[t] for t in range(3)))
                down_spot = tuple((spot[t] - unit_i[t] for t in range(3)))
                flux = at_shift(coeffs[comp], spot) * (
                    0.5 * (at_shift(padded, up_spot) - at_shift(padded, down_spot))
                )
                total = total + 0.5 * sign * flux
    return total


def add_misfit(field, column, sensor_cells, start_cell):
    count = field.shape[0]
    cells = field.shape[1] * field.shape[2] * field.shape[3]
    local = sensor_cells - start_cell
    positions = lax.broadcasted_iota(jnp.int32, (count, cells), 1)
    hit = positions == local[:, None]
    return field + jnp.where(hit, column[:, None], 0.0).reshape(field.shape)


def body(
    adjoint_end,
    checkpoints,
    dispersion,
    owner_steps,
    sensor_cells,
    misfit,
    release_cells,
    release_steps,
):
    own_sensors, depth, rows_y, rows_x = adjoint_end.shape
    slot_count = checkpoints.shape[0]
    cells = depth * rows_y * rows_x
    first_cell = lax.axis_index("space") * cells
    release_local = release_cells - first_cell
    release_inside = (release_local >= 0) & (release_local < cells)
    release_index = jnp.clip(release_local, 0, cells - 1)
    lam = adjoint_end
    partial_grad = jnp.zeros((own_sensors, release_cells.shape[0]), jnp.float32)
    whole = lax.all_gather(dispersion, "sens", axis=2, tiled=True)
    tensor = extended(whole, (("space", 1),), 1)
    for step in reversed(range(STEPS)):
        holder = owner_steps[step] // slot_count
        mine = lax.dynamic_index_in_dim(
            checkpoints, owner_steps[step] % slot_count, 0, keepdims=False
        )
        conc = broadcast(mine, "sens", holder)
        mixed = add_misfit(lam, misfit[:, step], sensor_cells, first_cell)
        scaled = retard_scale(conc) * mixed
        stacked = jnp.concatenate([conc[None], scaled], 0)
        rimmed = extended(stacked, (("space", 1),), 1)
        applied = apply_op(rimmed, tensor)
        lam = mixed + applied[1:] + retard_slope(conc) * applied[0] * mixed
        values = jnp.take(lam.reshape(own_sensors, cells), release_index, axis=1)
        keep = release_inside & (release_steps == step)
        partial_grad = partial_grad + jnp.where(keep[None, :], values, 0.0)
    release_grad = lax.psum(partial_grad, "space")
    return (lam, release_grad)


def solution(mesh):
    in_specs = (
        P("sens", "space", None, None),
        P("sens", "space", None, None),
        P(None, "space", "sens", None),
        P(),
        P("sens"),
        P("sens", None),
        P(),
        P(),
    )
    out_specs = (P("sens", "space", None, None), P("sens", None))
    return jax.shard_map(body, mesh=mesh, in_specs=in_specs, out_specs=out_specs, check_vma=False)
```

profile of v0, /device:TPU:0, one launch (start us, length us, event | category | flops | bytes accessed | tf_op | source)
XLA Modules:
  0.0 248.9 jit_solution(358271755512530131)
XLA Ops:
  7.2 0.0 all-reduce.7.cloned.1.call-start
  7.2 2.8 %all_gather.3 = f32[6,4,64,128]{3,2,1,0:T(8,128)S(1)} all-gather(f32[6,4,32,128]{3,2,1,0:T(8,128)} %param.12), channel_id=1, replica_groups=mesh['space'=16,'sens'=2] {'sens'}, dimensions={2}, use_global_device_ids=true | all-gather | bytes 1179648 | tf_op jit(solution)/shard_map/all_gather | solution.py:107
  10.1 4.8 %collective-permute-start = (f32[6,1,64,128]{3,2,1,0:T(8,128)S(1)}, f32[6,1,64,128]{3,2,1,0:T(8,128)S(1)}, u32[]{:S(2)}, u32[]{:S(2)}) collective-permute-start(f32[6,1,64,128]{3,2,1,0:T(8,128)S(1)} %get-tuple-element.28), channel_id=1, source_target_pairs={{0,2},{2,4},{4,6},{6,8},{8,10},{10,12},{12,14},{14,16},{16,18},{18... | collective-permute-start | bytes 589832 | tf_op jit(solution)/shard_map/ppermute | solution.py:15
  14.8 1.3 collective-permute-start.1
  16.2 0.6 fusion.113
  24.6 0.8 select_bitcast_fusion
  25.3 0.0 all-reduce.7.cloned.1.call-update
  25.4 0.0 copy-done.58
  25.4 0.0 collective-permute-done
  25.4 0.0 collective-permute-done.1
  25.5 0.8 select_maximum_fusion.9
  26.2 1.2 slice_bitcast_fusion.5
  27.4 1.0 slice_multiply_fusion.11
  28.5 0.3 slice_multiply_fusion.3
  28.8 17.7 %all-reduce.7.cloned.1.call-done = (f32[4,64,128]{2,1,0:T(8,128)}, f32[4,64,128]{2,1,0:T(8,128)}, f32[4,64,128]{2,1,0:T(8,128)}) async-done(((f32[4,64,128]{2,1,0:T(8,128)}, f32[4,64,128]{2,1,0:T(8,128)}, f32[4,64,128]{2,1,0:T(8,128)}), (f32[4,64,128]{2,1,0:T(8,128)}, f32[4,64,128]{2,1,0:T(8,128)}, f32[4,64,128]{2,1,0:T(8,128)})) %all-reduce.7.cloned.1.call-update) | async-done | bytes 393232 | tf_op jit(solution)/shard_map/psum | solution.py:25
  46.5 1.0 fusion.107
  47.5 0.3 fusion.89
  47.8 0.0 copy-start.48
  47.8 0.6 copy-done.4
  48.4 3.7 %collective-permute-start.3 = (f32[9,1,64,128]{3,2,1,0:T(8,128)S(1)}, f32[9,1,64,128]{3,2,1,0:T(8,128)S(1)}, u32[]{:S(2)}, u32[]{:S(2)}) collective-permute-start(f32[9,1,64,128]{3,2,1,0:T(8,128)S(1)} %get-tuple-element.26), channel_id=1, source_target_pairs={{0,2},{2,4},{4,6},{6,8},{8,10},{10,12},{12,14},{14,16},{16,18},{18... | collective-permute-start | bytes 884744 | tf_op jit(solution)/shard_map/ppermute | solution.py:15
  52.1 1.3 collective-permute-start.2
  53.4 0.0 copy-done.48
  53.4 0.0 copy-done.49
  53.5 0.3 fusion.102
  53.8 0.1 fusion.106
  53.9 11.3 %collective-permute-done.3 = f32[9,1,64,128]{3,2,1,0:T(8,128)S(1)} collective-permute-done((f32[9,1,64,128]{3,2,1,0:T(8,128)S(1)}, f32[9,1,64,128]{3,2,1,0:T(8,128)S(1)}, u32[]{:S(2)}, u32[]{:S(2)}) %collective-permute-start.3) | collective-permute-done | bytes 294944 | tf_op jit(solution)/shard_map/ppermute | solution.py:15
  65.1 1.9 collective-permute-done.2
  67.1 2.7 %select_maximum_fusion.6 = f32[9,6,66,130]{3,2,1,0:T(8,128)S(1)} fusion(f32[9,1,64,128]{3,2,1,0:T(8,128)S(1)} %collective-permute-done.2, f32[9,1,64,128]{3,2,1,0:T(8,128)S(1)} %collective-permute-done.3, f32[8,4,64,128]{3,2,1,0:T(8,128)S(1)} %fusion.89, f32[1,4,64,128]{3,2,1,0:T(8,128)S(1)} %bitcast.69), kind=kLoop, calls=%fused_computation.13 | loop fusion | flops 8339760 | bytes 3622752 | tf_op jit(solution)/shard_map/concatenate | solution.py:19
  69.9 4.7 %fusion.69 = f32[9,4,64,128]{3,2,1,0:T(8,128)S(1)} fusion(f32[9,6,66,130]{3,2,1,0:T(8,128)S(1)} %select_maximum_fusion.6, f32[9,1,64,128]{3,2,1,0:T(8,128)S(1)} %collective-permute-done.3, f32[8,4,64,128]{3,2,1,0:T(8,128)S(1)} %fusion.89, f32[1,4,64,128]{3,2,1,0:T(8,128)S(1)} %bitcast.70, f32[9,1,64,128]{3,2,1,0:T(8,128)S(1)} %collective-permute-done.2, ...), kind=kLoop, calls=%fused_computation.120 | loop fusion | flops 20643840 | bytes 24182784 | tf_op jit(solution)/shard_map/add | solution.py:75
  74.5 0.1 fusion.98
  74.6 0.6 fusion.88
  75.2 0.0 copy-start.57
  75.2 0.0 copy-start.59
  75.3 3.4 %collective-permute-start.5 = (f32[9,1,64,128]{3,2,1,0:T(8,128)S(1)}, f32[9,1,64,128]{3,2,1,0:T(8,128)S(1)}, u32[]{:S(2)}, u32[]{:S(2)}) collective-permute-start(f32[9,1,64,128]{3,2,1,0:T(8,128)S(1)} %get-tuple-element.24), channel_id=1, source_target_pairs={{0,2},{2,4},{4,6},{6,8},{8,10},{10,12},{12,14},{14,16},{16,18},{18... | collective-permute-start | bytes 884744 | tf_op jit(solution)/shard_map/ppermute | solution.py:15
  78.7 1.5 collective-permute-start.4
  80.2 0.6 compare_and_fusion.3
  80.8 0.1 fusion.105
  80.9 10.0 %collective-permute-done.5 = f32[9,1,64,128]{3,2,1,0:T(8,128)S(1)} collective-permute-done((f32[9,1,64,128]{3,2,1,0:T(8,128)S(1)}, f32[9,1,64,128]{3,2,1,0:T(8,128)S(1)}, u32[]{:S(2)}, u32[]{:S(2)}) %collective-permute-start.5) | collective-permute-done | bytes 294944 | tf_op jit(solution)/shard_map/ppermute | solution.py:15
  90.9 0.7 collective-permute-done.4
  91.6 2.7 %select_maximum_fusion.3 = f32[9,6,66,130]{3,2,1,0:T(8,128)S(1)} fusion(f32[9,1,64,128]{3,2,1,0:T(8,128)S(1)} %collective-permute-done.4, f32[9,1,64,128]{3,2,1,0:T(8,128)S(1)} %collective-permute-done.5, f32[8,4,64,128]{3,2,1,0:T(8,128)S(1)} %get-tuple-element.14, f32[1,4,64,128]{3,2,1,0:T(8,128)S(1)} %bitcast.66), kind=kLoop, calls=%fused_computation.10 | loop fusion | flops 8339760 | bytes 3622752 | tf_op jit(solution)/shard_map/concatenate | solution.py:19
  94.4 4.7 %fusion.44 = f32[9,4,64,128]{3,2,1,0:T(8,128)S(1)} fusion(f32[9,6,66,130]{3,2,1,0:T(8,128)S(1)} %select_maximum_fusion.3, f32[9,1,64,128]{3,2,1,0:T(8,128)S(1)} %collective-permute-done.5, f32[8,4,64,128]{3,2,1,0:T(8,128)S(1)} %get-tuple-element.14, f32[1,4,64,128]{3,2,1,0:T(8,128)S(1)} %bitcast.67, f32[9,1,64,128]{3,2,1,0:T(8,128)S(1)} %collective-permute-done.4, ...), kind=kLoop, calls=%fused_computation.87 | loop fusion | flops 20643840 | bytes 24182784 | tf_op jit(solution)/shard_map/add | solution.py:75
  99.1 0.1 fusion.97
  99.2 0.6 fusion.87
  99.8 0.8 fusion.91
  100.6 4.3 %collective-permute-start.7 = (f32[9,1,64,128]{3,2,1,0:T(8,128)}, f32[9,1,64,128]{3,2,1,0:T(8,128)}, u32[]{:S(2)}, u32[]{:S(2)}) collective-permute-start(f32[9,1,64,128]{3,2,1,0:T(8,128)} %get-tuple-element.22), channel_id=1, source_target_pairs={{0,2},{2,4},{4,6},{6,8},{8,10},{10,12},{12,14},{14,16},{16,18},{18... | collective-permute-start | bytes 884744 | tf_op jit(solution)/shard_map/ppermute | solution.py:15
  105.0 1.3 collective-permute-start.6
  106.3 0.5 compare_and_fusion.2
  106.8 8.7 %copy.10 = f32[8,4,64,128]{0,3,2,1:T(8,128)} copy(f32[8,4,64,128]{3,2,1,0:T(8,128)S(1)} %get-tuple-element.15) | data formatting | bytes 2097152 | tf_op jit(solution)/shard_map/add | solution.py:120
  115.5 7.0 %gather_fusion = f32[128,8]{1,0:T(8,128)} fusion(f32[8,32768]{0,1:T(8,128)} %bitcast.59, s32[1024]{0:T(1024)S(1)} %pad_clamp_fusion), kind=kCustom, calls=%fused_computation.clone | custom fusion | bytes 8704 | tf_op jit(solution)/shard_map/jit(_take)/gather | solution.py:121
  122.5 8.7 %copy.11 = f32[8,4,64,128]{0,3,2,1:T(8,128)} copy(f32[8,4,64,128]{3,2,1,0:T(8,128)S(1)} %get-tuple-element.13) | data formatting | bytes 2097152 | tf_op jit(solution)/shard_map/add | solution.py:120
  131.1 7.0 %gather_fusion.1 = f32[128,8]{1,0:T(8,128)} fusion(f32[8,32768]{0,1:T(8,128)} %bitcast.61, s32[1024]{0:T(1024)S(1)} %pad_clamp_fusion), kind=kCustom, calls=%fused_computation.1.clone | custom fusion | bytes 8704 | tf_op jit(solution)/shard_map/jit(_take)/gather | solution.py:121
  138.3 0.0 collective-permute-done.7
  138.3 0.0 collective-permute-done.6
  138.3 3.9 %select_maximum_fusion = f32[9,6,66,130]{3,2,1,0:T(8,128)S(1)} fusion(f32[9,1,64,128]{3,2,1,0:T(8,128)} %collective-permute-done.6, f32[9,1,64,128]{3,2,1,0:T(8,128)} %collective-permute-done.7, f32[8,4,64,128]{3,2,1,0:T(8,128)S(1)} %get-tuple-element.12, f32[1,4,64,128]{3,2,1,0:T(8,128)S(1)} %bitcast.63), kind=kLoop, calls=%fused_computation.7 | loop fusion | flops 8339760 | bytes 3622752 | tf_op jit(solution)/shard_map/concatenate | solution.py:19
  142.4 5.7 %fusion.19 = f32[9,4,64,128]{3,2,1,0:T(8,128)S(1)} fusion(f32[9,6,66,130]{3,2,1,0:T(8,128)S(1)} %select_maximum_fusion, f32[9,1,64,128]{3,2,1,0:T(8,128)} %collective-permute-done.7, f32[8,4,64,128]{3,2,1,0:T(8,128)S(1)} %get-tuple-element.12, f32[1,4,64,128]{3,2,1,0:T(8,128)S(1)} %bitcast.64, f32[9,1,64,128]{3,2,1,0:T(8,128)} %collective-permute-done.6, ...), kind=kLoop, calls=%fused_computation.54 | loop fusion | flops 20643840 | bytes 24182784 | tf_op jit(solution)/shard_map/add | solution.py:75
  148.1 0.1 fusion.96
  148.2 0.4 fusion.84
  148.6 0.0 copy-start
  148.6 0.0 copy-start.54
  148.6 8.7 %copy.12 = f32[8,4,64,128]{0,3,2,1:T(8,128)} copy(f32[8,4,64,128]{3,2,1,0:T(8,128)S(1)} %fusion.84) | data formatting | bytes 2097152 | tf_op jit(solution)/shard_map/add | solution.py:120
  157.4 6.4 %gather_fusion.2 = f32[128,8]{1,0:T(8,128)S(1)} fusion(f32[8,32768]{0,1:T(8,128)} %bitcast.60, s32[1024]{0:T(1024)S(1)} %pad_clamp_fusion), kind=kCustom, calls=%fused_computation.2.clone | custom fusion | bytes 8704 | tf_op jit(solution)/shard_map/jit(_take)/gather | solution.py:121
  163.8 0.1 fusion.108
  164.0 77.5 %psum.31 = f32[8,128]{0,1:T(8,128)S(1)} all-reduce(f32[8,128]{0,1:T(8,128)S(1)} %fusion.108), channel_id=1, replica_groups=mesh['space'=16,'sens'=2] {'space'}, use_global_device_ids=true, to_apply=%region_3.5 | all-reduce | flops 1024 | bytes 8192 | tf_op jit(solution)/shard_map/psum | solution.py:124
  241.4 0.7 copy.13
  (120 shorter events, 0.4 us)
Async XLA Ops:
  7.2 9.0 %copy-start.53 = (s32[3]{0:T(128)S(1)}, s32[3]{0:T(128)}, u32[]{:S(2)}) copy-start(s32[3]{0:T(128)} %param.13) | copy-start | bytes 40
  7.2 17.4 %copy-start.50 = (f32[4,4,64,128]{3,2,1,0:T(8,128)S(1)}, f32[4,4,64,128]{3,2,1,0:T(8,128)}, u32[]{:S(2)}) copy-start(f32[4,4,64,128]{3,2,1,0:T(8,128)} %param.11) | copy-start | bytes 1572868
  7.2 39.3 %all-reduce.7.cloned.1.call-start = ((), (), s32[]{:S(2)}) async-start(), calls=%async_computation | async-start | bytes 786432 | tf_op jit(solution)/shard_map/psum | solution.py:25
  10.0 15.4 %copy-start.58 = (f32[8,3]{0,1:T(4,128)S(1)}, f32[8,3]{0,1:T(4,128)}, u32[]{:S(2)}) copy-start(f32[8,3]{0,1:T(4,128)} %param.15) | copy-start | bytes 292
  10.0 15.4 %copy-start.60 = (s32[8]{0:T(128)S(1)}, s32[8]{0:T(128)}, u32[]{:S(2)}) copy-start(s32[8]{0:T(128)} %param.14) | copy-start | bytes 100
  10.1 15.4 %collective-permute-start = (f32[6,1,64,128]{3,2,1,0:T(8,128)S(1)}, f32[6,1,64,128]{3,2,1,0:T(8,128)S(1)}, u32[]{:S(2)}, u32[]{:S(2)}) collective-permute-start(f32[6,1,64,128]{3,2,1,0:T(8,128)S(1)} %get-tuple-element.28), channel_id=1, source_target_pairs={{0,2},{2,4},{4,6},{6,8},{8,10},{10,12},{12,14},{14,16},{16,18},{18... | collective-permute-start | bytes 589832 | tf_op jit(solution)/shard_map/ppermute | solution.py:15
  14.8 10.6 %collective-permute-start.1 = (f32[6,1,64,128]{3,2,1,0:T(8,128)S(1)}, f32[6,1,64,128]{3,2,1,0:T(8,128)S(1)}, u32[]{:S(2)}, u32[]{:S(2)}) collective-permute-start(f32[6,1,64,128]{3,2,1,0:T(8,128)S(1)} %get-tuple-element.29), channel_id=1, source_target_pairs={{2,0},{4,2},{6,4},{8,6},{10,8},{12,10},{14,12},{16,14},{18,16},{20... | collective-permute-start | bytes 589832 | tf_op jit(solution)/shard_map/ppermute | solution.py:18
  28.4 41.3 %copy-start.33 = (f32[4,64,128]{2,1,0:T(8,128)}, f32[4,64,128]{2,1,0:T(8,128)S(1)}, u32[]{:S(2)}) copy-start(f32[4,64,128]{2,1,0:T(8,128)S(1)} %get-tuple-element.39) | copy-start | bytes 393220
  28.5 41.3 %copy-start.36 = (f32[4,64,128]{2,1,0:T(8,128)}, f32[4,64,128]{2,1,0:T(8,128)S(1)}, u32[]{:S(2)}) copy-start(f32[4,64,128]{2,1,0:T(8,128)S(1)} %get-tuple-element.40) | copy-start | bytes 393220
  28.5 41.3 %copy-start.39 = (f32[4,64,128]{2,1,0:T(8,128)}, f32[4,64,128]{2,1,0:T(8,128)S(1)}, u32[]{:S(2)}) copy-start(f32[4,64,128]{2,1,0:T(8,128)S(1)} %get-tuple-element.41) | copy-start | bytes 393220
  28.5 19.0 %copy-start.1 = (f32[8,4,64,128]{3,2,1,0:T(8,128)S(1)}, f32[8,4,64,128]{3,2,1,0:T(8,128)}, u32[]{:S(2)}) copy-start(f32[8,4,64,128]{3,2,1,0:T(8,128)} %param.10) | copy-start | bytes 3145732
  28.7 41.0 %copy-start.7 = (f32[4,64,128]{2,1,0:T(8,128)}, f32[4,64,128]{2,1,0:T(8,128)S(1)}, u32[]{:S(2)}) copy-start(f32[4,64,128]{2,1,0:T(8,128)S(1)} %get-tuple-element.49) | copy-start | bytes 393220
  28.8 41.0 %copy-start.10 = (f32[4,64,128]{2,1,0:T(8,128)}, f32[4,64,128]{2,1,0:T(8,128)S(1)}, u32[]{:S(2)}) copy-start(f32[4,64,128]{2,1,0:T(8,128)S(1)} %get-tuple-element.50) | copy-start | bytes 393220
  28.8 41.0 %copy-start.13 = (f32[4,64,128]{2,1,0:T(8,128)}, f32[4,64,128]{2,1,0:T(8,128)S(1)}, u32[]{:S(2)}) copy-start(f32[4,64,128]{2,1,0:T(8,128)S(1)} %get-tuple-element.61) | copy-start | bytes 393220
  28.8 41.0 %copy-start.16 = (f32[4,64,128]{2,1,0:T(8,128)}, f32[4,64,128]{2,1,0:T(8,128)S(1)}, u32[]{:S(2)}) copy-start(f32[4,64,128]{2,1,0:T(8,128)S(1)} %get-tuple-element.62) | copy-start | bytes 393220
  28.8 41.0 %copy-start.19 = (f32[4,64,128]{2,1,0:T(8,128)}, f32[4,64,128]{2,1,0:T(8,128)S(1)}, u32[]{:S(2)}) copy-start(f32[4,64,128]{2,1,0:T(8,128)S(1)} %get-tuple-element.63) | copy-start | bytes 393220
  28.8 41.0 %copy-start.22 = (f32[4,64,128]{2,1,0:T(8,128)}, f32[4,64,128]{2,1,0:T(8,128)S(1)}, u32[]{:S(2)}) copy-start(f32[4,64,128]{2,1,0:T(8,128)S(1)} %get-tuple-element.64) | copy-start | bytes 393220
  28.8 65.5 %copy-start.5 = (f32[4,64,128]{2,1,0:T(8,128)}, f32[4,64,128]{2,1,0:T(8,128)S(1)}, u32[]{:S(2)}) copy-start(f32[4,64,128]{2,1,0:T(8,128)S(1)} %get-tuple-element.48) | copy-start | bytes 393220
  47.8 5.7 %copy-start.48 = (f32[6,66,130]{2,1,0:T(8,128)S(1)}, f32[6,66,130]{2,1,0:T(8,128)}, u32[]{:S(2)}) copy-start(f32[6,66,130]{2,1,0:T(8,128)} %get-tuple-element.16) | copy-start | bytes 617764
  47.8 5.7 %copy-start.49 = (f32[6,66,130]{2,1,0:T(8,128)S(1)}, f32[6,66,130]{2,1,0:T(8,128)}, u32[]{:S(2)}) copy-start(f32[6,66,130]{2,1,0:T(8,128)} %get-tuple-element.20) | copy-start | bytes 617764
  48.4 5.4 %copy-start.3 = (f32[4,64,128]{2,1,0:T(8,128)S(1)}, f32[4,64,128]{2,1,0:T(8,128)}, u32[]{:S(2)}) copy-start(f32[4,64,128]{2,1,0:T(8,128)} %get-tuple-element.6) | copy-start | bytes 393220
  48.4 16.7 %collective-permute-start.3 = (f32[9,1,64,128]{3,2,1,0:T(8,128)S(1)}, f32[9,1,64,128]{3,2,1,0:T(8,128)S(1)}, u32[]{:S(2)}, u32[]{:S(2)}) collective-permute-start(f32[9,1,64,128]{3,2,1,0:T(8,128)S(1)} %get-tuple-element.26), channel_id=1, source_target_pairs={{0,2},{2,4},{4,6},{6,8},{8,10},{10,12},{12,14},{14,16},{16,18},{18... | collective-permute-start | bytes 884744 | tf_op jit(solution)/shard_map/ppermute | solution.py:15
  52.1 14.9 %collective-permute-start.2 = (f32[9,1,64,128]{3,2,1,0:T(8,128)S(1)}, f32[9,1,64,128]{3,2,1,0:T(8,128)S(1)}, u32[]{:S(2)}, u32[]{:S(2)}) collective-permute-start(f32[9,1,64,128]{3,2,1,0:T(8,128)S(1)} %get-tuple-element.27), channel_id=1, source_target_pairs={{2,0},{4,2},{6,4},{8,6},{10,8},{12,10},{14,12},{16,14},{18,16},{20... | collective-permute-start | bytes 884744 | tf_op jit(solution)/shard_map/ppermute | solution.py:18
  53.7 40.6 %copy-start.25 = (f32[4,64,128]{2,1,0:T(8,128)}, f32[4,64,128]{2,1,0:T(8,128)S(1)}, u32[]{:S(2)}) copy-start(f32[4,64,128]{2,1,0:T(8,128)S(1)} %get-tuple-element.35) | copy-start | bytes 393220
  53.7 40.6 %copy-start.27 = (f32[4,64,128]{2,1,0:T(8,128)}, f32[4,64,128]{2,1,0:T(8,128)S(1)}, u32[]{:S(2)}) copy-start(f32[4,64,128]{2,1,0:T(8,128)S(1)} %get-tuple-element.36) | copy-start | bytes 393220
  53.8 40.6 %copy-start.29 = (f32[4,64,128]{2,1,0:T(8,128)}, f32[4,64,128]{2,1,0:T(8,128)S(1)}, u32[]{:S(2)}) copy-start(f32[4,64,128]{2,1,0:T(8,128)S(1)} %get-tuple-element.67) | copy-start | bytes 393220
  53.8 40.6 %copy-start.31 = (f32[4,64,128]{2,1,0:T(8,128)}, f32[4,64,128]{2,1,0:T(8,128)S(1)}, u32[]{:S(2)}) copy-start(f32[4,64,128]{2,1,0:T(8,128)S(1)} %get-tuple-element.68) | copy-start | bytes 393220
  53.9 16.0 %copy-start.42 = (f32[4,64,128]{2,1,0:T(8,128)S(1)}, f32[4,64,128]{2,1,0:T(8,128)}, u32[]{:S(2)}) copy-start(f32[4,64,128]{2,1,0:T(8,128)} %get-tuple-element.42) | copy-start | bytes 393220
  53.9 16.0 %copy-start.44 = (f32[4,64,128]{2,1,0:T(8,128)S(1)}, f32[4,64,128]{2,1,0:T(8,128)}, u32[]{:S(2)}) copy-start(f32[4,64,128]{2,1,0:T(8,128)} %get-tuple-element.65) | copy-start | bytes 393220
  53.9 16.0 %copy-start.46 = (f32[4,64,128]{2,1,0:T(8,128)S(1)}, f32[4,64,128]{2,1,0:T(8,128)}, u32[]{:S(2)}) copy-start(f32[4,64,128]{2,1,0:T(8,128)} %get-tuple-element.66) | copy-start | bytes 393220
  75.2 5.0 %copy-start.57 = (s32[128]{0:T(128)S(1)}, s32[128]{0:T(128)}, u32[]{:S(2)}) copy-start(s32[128]{0:T(128)} %param.17) | copy-start | bytes 1540
  75.2 5.0 %copy-start.59 = (s32[128]{0:T(128)S(1)}, s32[128]{0:T(128)}, u32[]{:S(2)}) copy-start(s32[128]{0:T(128)} %param.16) | copy-start | bytes 1540
  75.2 5.5 %copy-start.2 = (f32[4,64,128]{2,1,0:T(8,128)S(1)}, f32[4,64,128]{2,1,0:T(8,128)}, u32[]{:S(2)}) copy-start(f32[4,64,128]{2,1,0:T(8,128)} %get-tuple-element.7) | copy-start | bytes 393220
  75.3 15.6 %collective-permute-start.5 = (f32[9,1,64,128]{3,2,1,0:T(8,128)S(1)}, f32[9,1,64,128]{3,2,1,0:T(8,128)S(1)}, u32[]{:S(2)}, u32[]{:S(2)}) collective-permute-start(f32[9,1,64,128]{3,2,1,0:T(8,128)S(1)} %get-tuple-element.24), channel_id=1, source_target_pairs={{0,2},{2,4},{4,6},{6,8},{8,10},{10,12},{12,14},{14,16},{16,18},{18... | collective-permute-start | bytes 884744 | tf_op jit(solution)/shard_map/ppermute | solution.py:15
  78.7 12.9 %collective-permute-start.4 = (f32[9,1,64,128]{3,2,1,0:T(8,128)S(1)}, f32[9,1,64,128]{3,2,1,0:T(8,128)S(1)}, u32[]{:S(2)}, u32[]{:S(2)}) collective-permute-start(f32[9,1,64,128]{3,2,1,0:T(8,128)S(1)} %get-tuple-element.25), channel_id=1, source_target_pairs={{2,0},{4,2},{6,4},{8,6},{10,8},{12,10},{14,12},{16,14},{18,16},{20... | collective-permute-start | bytes 884744 | tf_op jit(solution)/shard_map/ppermute | solution.py:18
  80.8 13.5 %copy-start.8 = (f32[4,64,128]{2,1,0:T(8,128)S(1)}, f32[4,64,128]{2,1,0:T(8,128)}, u32[]{:S(2)}) copy-start(f32[4,64,128]{2,1,0:T(8,128)} %copy-done.7) | copy-start | bytes 393220
  80.8 13.5 %copy-start.11 = (f32[4,64,128]{2,1,0:T(8,128)S(1)}, f32[4,64,128]{2,1,0:T(8,128)}, u32[]{:S(2)}) copy-start(f32[4,64,128]{2,1,0:T(8,128)} %copy-done.10) | copy-start | bytes 393220
  80.9 13.5 %copy-start.14 = (f32[4,64,128]{2,1,0:T(8,128)S(1)}, f32[4,64,128]{2,1,0:T(8,128)}, u32[]{:S(2)}) copy-start(f32[4,64,128]{2,1,0:T(8,128)} %copy-done.13) | copy-start | bytes 393220
  80.9 13.5 %copy-start.17 = (f32[4,64,128]{2,1,0:T(8,128)S(1)}, f32[4,64,128]{2,1,0:T(8,128)}, u32[]{:S(2)}) copy-start(f32[4,64,128]{2,1,0:T(8,128)} %copy-done.16) | copy-start | bytes 393220
  80.9 13.5 %copy-start.20 = (f32[4,64,128]{2,1,0:T(8,128)S(1)}, f32[4,64,128]{2,1,0:T(8,128)}, u32[]{:S(2)}) copy-start(f32[4,64,128]{2,1,0:T(8,128)} %copy-done.19) | copy-start | bytes 393220
  80.9 13.5 %copy-start.23 = (f32[4,64,128]{2,1,0:T(8,128)S(1)}, f32[4,64,128]{2,1,0:T(8,128)}, u32[]{:S(2)}) copy-start(f32[4,64,128]{2,1,0:T(8,128)} %copy-done.22) | copy-start | bytes 393220
  80.9 13.5 %copy-start.34 = (f32[4,64,128]{2,1,0:T(8,128)S(1)}, f32[4,64,128]{2,1,0:T(8,128)}, u32[]{:S(2)}) copy-start(f32[4,64,128]{2,1,0:T(8,128)} %copy-done.33) | copy-start | bytes 393220
  80.9 13.5 %copy-start.37 = (f32[4,64,128]{2,1,0:T(8,128)S(1)}, f32[4,64,128]{2,1,0:T(8,128)}, u32[]{:S(2)}) copy-start(f32[4,64,128]{2,1,0:T(8,128)} %copy-done.36) | copy-start | bytes 393220
  80.9 13.5 %copy-start.40 = (f32[4,64,128]{2,1,0:T(8,128)S(1)}, f32[4,64,128]{2,1,0:T(8,128)}, u32[]{:S(2)}) copy-start(f32[4,64,128]{2,1,0:T(8,128)} %copy-done.39) | copy-start | bytes 393220
  100.6 37.6 %collective-permute-start.7 = (f32[9,1,64,128]{3,2,1,0:T(8,128)}, f32[9,1,64,128]{3,2,1,0:T(8,128)}, u32[]{:S(2)}, u32[]{:S(2)}) collective-permute-start(f32[9,1,64,128]{3,2,1,0:T(8,128)} %get-tuple-element.22), channel_id=1, source_target_pairs={{0,2},{2,4},{4,6},{6,8},{8,10},{10,12},{12,14},{14,16},{16,18},{18... | collective-permute-start | bytes 884744 | tf_op jit(solution)/shard_map/ppermute | solution.py:15
  105.0 33.3 %collective-permute-start.6 = (f32[9,1,64,128]{3,2,1,0:T(8,128)}, f32[9,1,64,128]{3,2,1,0:T(8,128)}, u32[]{:S(2)}, u32[]{:S(2)}) collective-permute-start(f32[9,1,64,128]{3,2,1,0:T(8,128)} %get-tuple-element.23), channel_id=1, source_target_pairs={{2,0},{4,2},{6,4},{8,6},{10,8},{12,10},{14,12},{16,14},{18,16},{20... | collective-permute-start | bytes 884744 | tf_op jit(solution)/shard_map/ppermute | solution.py:18
  138.1 4.1 %copy-start.18 = (f32[4,64,128]{2,1,0:T(8,128)S(1)}, f32[4,64,128]{2,1,0:T(8,128)}, u32[]{:S(2)}) copy-start(f32[4,64,128]{2,1,0:T(8,128)} %copy-done.16) | copy-start | bytes 393220
  138.1 4.1 %copy-start.21 = (f32[4,64,128]{2,1,0:T(8,128)S(1)}, f32[4,64,128]{2,1,0:T(8,128)}, u32[]{:S(2)}) copy-start(f32[4,64,128]{2,1,0:T(8,128)} %copy-done.19) | copy-start | bytes 393220
  138.1 4.1 %copy-start.24 = (f32[4,64,128]{2,1,0:T(8,128)S(1)}, f32[4,64,128]{2,1,0:T(8,128)}, u32[]{:S(2)}) copy-start(f32[4,64,128]{2,1,0:T(8,128)} %copy-done.22) | copy-start | bytes 393220
  138.2 4.1 %copy-start.26 = (f32[4,64,128]{2,1,0:T(8,128)S(1)}, f32[4,64,128]{2,1,0:T(8,128)}, u32[]{:S(2)}) copy-start(f32[4,64,128]{2,1,0:T(8,128)} %copy-done.25) | copy-start | bytes 393220
  138.2 4.1 %copy-start.28 = (f32[4,64,128]{2,1,0:T(8,128)S(1)}, f32[4,64,128]{2,1,0:T(8,128)}, u32[]{:S(2)}) copy-start(f32[4,64,128]{2,1,0:T(8,128)} %copy-done.27) | copy-start | bytes 393220
  138.2 4.1 %copy-start.30 = (f32[4,64,128]{2,1,0:T(8,128)S(1)}, f32[4,64,128]{2,1,0:T(8,128)}, u32[]{:S(2)}) copy-start(f32[4,64,128]{2,1,0:T(8,128)} %copy-done.29) | copy-start | bytes 393220
  138.2 4.1 %copy-start.32 = (f32[4,64,128]{2,1,0:T(8,128)S(1)}, f32[4,64,128]{2,1,0:T(8,128)}, u32[]{:S(2)}) copy-start(f32[4,64,128]{2,1,0:T(8,128)} %copy-done.31) | copy-start | bytes 393220
  138.2 4.1 %copy-start.35 = (f32[4,64,128]{2,1,0:T(8,128)S(1)}, f32[4,64,128]{2,1,0:T(8,128)}, u32[]{:S(2)}) copy-start(f32[4,64,128]{2,1,0:T(8,128)} %copy-done.33) | copy-start | bytes 393220
  138.2 4.1 %copy-start.38 = (f32[4,64,128]{2,1,0:T(8,128)S(1)}, f32[4,64,128]{2,1,0:T(8,128)}, u32[]{:S(2)}) copy-start(f32[4,64,128]{2,1,0:T(8,128)} %copy-done.36) | copy-start | bytes 393220
  138.2 4.1 %copy-start.41 = (f32[4,64,128]{2,1,0:T(8,128)S(1)}, f32[4,64,128]{2,1,0:T(8,128)}, u32[]{:S(2)}) copy-start(f32[4,64,128]{2,1,0:T(8,128)} %copy-done.39) | copy-start | bytes 393220
  138.2 4.1 %copy-start.43 = (f32[4,64,128]{2,1,0:T(8,128)S(1)}, f32[4,64,128]{2,1,0:T(8,128)}, u32[]{:S(2)}) copy-start(f32[4,64,128]{2,1,0:T(8,128)} %get-tuple-element.42) | copy-start | bytes 393220
  138.2 4.1 %copy-start.45 = (f32[4,64,128]{2,1,0:T(8,128)S(1)}, f32[4,64,128]{2,1,0:T(8,128)}, u32[]{:S(2)}) copy-start(f32[4,64,128]{2,1,0:T(8,128)} %get-tuple-element.65) | copy-start | bytes 393220
  148.6 8.8 %copy-start = (f32[8,4,64,128]{3,2,1,0:T(8,128)}, f32[8,4,64,128]{3,2,1,0:T(8,128)S(1)}, u32[]{:S(2)}) copy-start(f32[8,4,64,128]{3,2,1,0:T(8,128)S(1)} %fusion.84) | copy-start | bytes 3145732
  148.6 15.2 %copy-start.51 = (f32[128,8]{1,0:T(8,128)S(1)}, f32[128,8]{1,0:T(8,128)}, u32[]{:S(2)}) copy-start(f32[128,8]{1,0:T(8,128)} %gather_fusion) | copy-start | bytes 12292
  148.6 15.2 %copy-start.52 = (f32[128,8]{1,0:T(8,128)S(1)}, f32[128,8]{1,0:T(8,128)}, u32[]{:S(2)}) copy-start(f32[128,8]{1,0:T(8,128)} %gather_fusion.1) | copy-start | bytes 12292
  148.6 15.2 %copy-start.54 = (pred[128]{0:T(512)(128)(4,1)S(1)}, pred[128]{0:T(512)(128)(4,1)}, u32[]{:S(2)}) copy-start(pred[128]{0:T(512)(128)(4,1)} %get-tuple-element.8) | copy-start | bytes 388
  148.6 15.2 %copy-start.55 = (pred[128]{0:T(512)(128)(4,1)S(1)}, pred[128]{0:T(512)(128)(4,1)}, u32[]{:S(2)}) copy-start(pred[128]{0:T(512)(128)(4,1)} %get-tuple-element.56) | copy-start | bytes 388
  148.6 15.2 %copy-start.56 = (pred[128]{0:T(512)(128)(4,1)S(1)}, pred[128]{0:T(512)(128)(4,1)}, u32[]{:S(2)}) copy-start(pred[128]{0:T(512)(128)(4,1)} %get-tuple-element.55) | copy-start | bytes 388
  (6 other events, 21.4 us)
Sparse Core Ops, SparseCore 0:
  25.5 20.9 all-reduce.6
where the time goes:
time: 250 us; the launch traced here: 249 us
  blocking collectives  80.2 us (32%)
  local copies, waits for them, and re-layouts  49.8 us (20%)
  waiting for transfers between devices  41.6 us (17%)
  other arithmetic  32.7 us (13%)
  between operations  23 us (9%)
  starting transfers between devices  21.6 us (9%)
    psum x1, blocking collectives, body(): release_grad = lax.psum(partial_grad, 'space')  77.5 us
    add x3, local copies, waits for them, and re-layouts, body(): lam = mixed + applied[1:] + retard_slope(conc) * applied[0] * mixed  26 us
    ppermute x4, waiting for transfers between devices, extended(): lax.ppermute(lax.slice_in_dim(block, block.shape[dim] - width, None, axis...  21.2 us
    gather x3, local copies, waits for them, and re-layouts, body(): values = jnp.take(lam.reshape(own_sensors, cells), release_index, axis=1)  20.4 us
    psum x1, waiting for transfers between devices, broadcast(): return lax.psum(jnp.where(mine, array, jnp.zeros_like(array)), axis)  17.7 us
    ppermute x4, starting transfers between devices, extended(): lax.ppermute(lax.slice_in_dim(block, block.shape[dim] - width, None, axis...  16.2 us
    add x3, other arithmetic, apply_op(): total = total + 0.5 * sign * flux  15 us
    concatenate x4, other arithmetic, extended(): block = jnp.concatenate([low, block, high], axis=dim)  9.99 us
  transfers between devices with their start and end apart: 9, of which 5 were waited for; matrix products, arithmetic and copies ran while one was open for 15% of the time, Pallas kernels for 0%

commit v1 on v0

--- a/solution.py
+++ b/solution.py
@@ -22,7 +22,7 @@
 
 def broadcast(array, axis, root):
     mine = lax.axis_index(axis) == root
-    return lax.psum(jnp.where(mine, array, jnp.zeros_like(array)), axis)
+    return jnp.sum(lax.all_gather(jnp.where(mine, array, jnp.zeros_like(array)), axis), axis=0)
 
 
 def retard_scale(conc):

time: 250 us -> 225 us (0.900)
  waiting for transfers between devices: 41.6 us -> 15.2 us
  between operations: 23 us -> 9.71 us
  blocking collectives: 80.2 us -> 87.5 us
  other arithmetic: 32.7 us -> 39 us
    psum x1 -> x0, waiting for transfers between devices: 17.7 us -> none  [broadcast(): return lax.psum(jnp.where(mine, array, jnp.zeros_like(array)), axis)]
    ppermute x4, waiting for transfers between devices: 21.2 us -> 6.92 us  [extended(): lax.ppermute(lax.slice_in_dim(block, block.shape[dim] - width, None, axis...]
    all_gather x0 -> x3, blocking collectives: none -> 6.28 us  [broadcast(): lax.all_gather(jnp.where(mine, array, jnp.zeros_like(array)), axis)]
    ppermute x4, waiting for transfers between devices: 2.68 us -> 8.3 us  [extended(): lax.ppermute(lax.slice_in_dim(block, 0, width, axis=dim), axis, backward)]
    concatenate x4, other arithmetic: 9.99 us -> 13.1 us  [extended(): block = jnp.concatenate([low, block, high], axis=dim)]
  transfers between devices with their start and end apart: 9 -> 8, of which waited for: 5 -> 3; matrix products, arithmetic and copies ran while one was open for 15% -> 17% of each run, Pallas kernels for 0% -> 0%
where the time goes in v1:
time: 225 us; the launch traced here: 224 us
  blocking collectives  87.5 us (39%)
  local copies, waits for them, and re-layouts  49 us (22%)
  other arithmetic  39 us (17%)
  starting transfers between devices  23.7 us (11%)
  waiting for transfers between devices  15.2 us (7%)
  between operations  9.71 us (4%)
    psum x1, blocking collectives, body(): release_grad = lax.psum(partial_grad, 'space')  78.4 us
    add x3, local copies, waits for them, and re-layouts, body(): lam = mixed + applied[1:] + retard_slope(conc) * applied[0] * mixed  26 us
    gather x3, local copies, waits for them, and re-layouts, body(): values = jnp.take(lam.reshape(own_sensors, cells), release_index, axis=1)  20.4 us
    ppermute x4, starting transfers between devices, extended(): lax.ppermute(lax.slice_in_dim(block, block.shape[dim] - width, None, axis...  18.6 us
    add x3, other arithmetic, apply_op(): total = total + 0.5 * sign * flux  17.2 us
    concatenate x4, other arithmetic, extended(): block = jnp.concatenate([low, block, high], axis=dim)  13.1 us
    ppermute x4, waiting for transfers between devices, extended(): lax.ppermute(lax.slice_in_dim(block, 0, width, axis=dim), axis, backward)  8.3 us
    ppermute x4, waiting for transfers between devices, extended(): lax.ppermute(lax.slice_in_dim(block, block.shape[dim] - width, None, axis...  6.92 us
  transfers between devices with their start and end apart: 8, of which 3 were waited for; matrix products, arithmetic and copies ran while one was open for 17% of the time, Pallas kernels for 0%

profile of v1, /device:TPU:0, one launch (start us, length us, event | category | flops | bytes accessed | tf_op | source)
XLA Modules:
  0.0 224.1 jit_solution(16900188747832690656)
XLA Ops:
  0.7 2.8 %all_gather.15 = f32[6,4,64,128]{3,2,1,0:T(8,128)S(1)} all-gather(f32[6,4,32,128]{3,2,1,0:T(8,128)} %param.12), channel_id=1, replica_groups=mesh['space'=16,'sens'=2] {'sens'}, dimensions={2}, use_global_device_ids=true | all-gather | bytes 1179648 | tf_op jit(solution)/shard_map/all_gather | solution.py:107
  3.5 0.8 fusion.109
  4.2 5.6 %collective-permute-start = (f32[6,1,64,128]{3,2,1,0:T(8,128)}, f32[6,1,64,128]{3,2,1,0:T(8,128)}, u32[]{:S(2)}, u32[]{:S(2)}) collective-permute-start(f32[6,1,64,128]{3,2,1,0:T(8,128)} %get-tuple-element.27), channel_id=1, source_target_pairs={{0,2},{2,4},{4,6},{6,8},{8,10},{10,12},{12,14},{14,16},{16,18},{18... | collective-permute-start | bytes 589832 | tf_op jit(solution)/shard_map/ppermute | solution.py:15
  9.8 1.3 collective-permute-start.1
  11.1 0.6 fusion.110
  19.6 0.7 dynamic-slice_select_fusion.2
  20.3 2.0 all_gather.16
  22.3 0.1 add_divide_fusion.2
  22.4 0.3 fusion.89
  22.7 0.0 copy-start.57
  22.7 0.0 copy-start.61
  22.7 0.9 fusion.95
  23.6 5.3 %collective-permute-start.3 = (f32[9,1,64,128]{3,2,1,0:T(8,128)}, f32[9,1,64,128]{3,2,1,0:T(8,128)}, u32[]{:S(2)}, u32[]{:S(2)}) collective-permute-start(f32[9,1,64,128]{3,2,1,0:T(8,128)} %get-tuple-element.25), channel_id=1, source_target_pairs={{0,2},{2,4},{4,6},{6,8},{8,10},{10,12},{12,14},{14,16},{16,18},{18... | collective-permute-start | bytes 884744 | tf_op jit(solution)/shard_map/ppermute | solution.py:15
  28.9 1.3 collective-permute-start.2
  30.2 2.0 all_gather.17
  32.2 0.1 add_divide_fusion.1
  32.3 0.6 compare_and_fusion.3
  32.9 0.0 collective-permute-done
  32.9 0.0 collective-permute-done.1
  32.9 1.8 select_maximum_fusion.9
  34.7 0.3 slice_bitcast_fusion.5
  34.9 0.3 slice_multiply_fusion.14
  35.3 0.3 fusion.102
  35.6 0.3 slice_multiply_fusion.6
  35.9 0.0 collective-permute-done.3
  35.9 7.6 %collective-permute-done.2 = f32[9,1,64,128]{3,2,1,0:T(8,128)} collective-permute-done((f32[9,1,64,128]{3,2,1,0:T(8,128)}, f32[9,1,64,128]{3,2,1,0:T(8,128)}, u32[]{:S(2)}, u32[]{:S(2)}) %collective-permute-start.2) | collective-permute-done | bytes 294944 | tf_op jit(solution)/shard_map/ppermute | solution.py:18
  43.5 3.7 %select_maximum_fusion.6 = f32[9,6,66,130]{3,2,1,0:T(8,128)S(1)} fusion(f32[9,1,64,128]{3,2,1,0:T(8,128)} %collective-permute-done.2, f32[9,1,64,128]{3,2,1,0:T(8,128)} %collective-permute-done.3, f32[8,4,64,128]{3,2,1,0:T(8,128)S(1)} %fusion.89, f32[1,4,64,128]{3,2,1,0:T(8,128)S(1)} %bitcast.57), kind=kLoop, calls=%fused_computation.13 | loop fusion | flops 8339760 | bytes 3622752 | tf_op jit(solution)/shard_map/concatenate | solution.py:19
  47.4 0.0 copy-start.2
  47.4 5.8 %fusion.69 = f32[9,4,64,128]{3,2,1,0:T(8,128)S(1)} fusion(f32[9,6,66,130]{3,2,1,0:T(8,128)S(1)} %select_maximum_fusion.6, f32[9,1,64,128]{3,2,1,0:T(8,128)} %collective-permute-done.3, f32[8,4,64,128]{3,2,1,0:T(8,128)S(1)} %fusion.89, f32[1,4,64,128]{3,2,1,0:T(8,128)S(1)} %bitcast.58, f32[9,1,64,128]{3,2,1,0:T(8,128)} %collective-permute-done.2, ...), kind=kLoop, calls=%fused_computation.120 | loop fusion | flops 20643840 | bytes 24182784 | tf_op jit(solution)/shard_map/add | solution.py:75
  53.2 0.1 fusion.98
  53.3 0.6 fusion.88
  53.9 0.9 fusion.93
  54.7 3.2 %collective-permute-start.5 = (f32[9,1,64,128]{3,2,1,0:T(8,128)}, f32[9,1,64,128]{3,2,1,0:T(8,128)}, u32[]{:S(2)}, u32[]{:S(2)}) collective-permute-start(f32[9,1,64,128]{3,2,1,0:T(8,128)} %get-tuple-element.23), channel_id=1, source_target_pairs={{0,2},{2,4},{4,6},{6,8},{8,10},{10,12},{12,14},{14,16},{16,18},{18... | collective-permute-start | bytes 884744 | tf_op jit(solution)/shard_map/ppermute | solution.py:15
  57.9 1.3 collective-permute-start.4
  59.2 2.3 %all_gather.18 = f32[2,4,64,128]{3,2,1,0:T(8,128)} all-gather(f32[1,4,64,128]{3,2,1,0:T(8,128)S(1)} %copy-done.48), channel_id=1, replica_groups=mesh['space'=16,'sens'=2] {'sens'}, dimensions={0}, use_global_device_ids=true | all-gather | bytes 393216 | tf_op jit(solution)/shard_map/all_gather | solution.py:25
  61.5 1.0 reduce_sum.29
  62.5 0.1 add_divide_fusion
  62.7 6.9 %collective-permute-done.5 = f32[9,1,64,128]{3,2,1,0:T(8,128)} collective-permute-done((f32[9,1,64,128]{3,2,1,0:T(8,128)}, f32[9,1,64,128]{3,2,1,0:T(8,128)}, u32[]{:S(2)}, u32[]{:S(2)}) %collective-permute-start.5) | collective-permute-done | bytes 294944 | tf_op jit(solution)/shard_map/ppermute | solution.py:15
  69.6 0.7 collective-permute-done.4
  70.3 3.7 %select_maximum_fusion.3 = f32[9,6,66,130]{3,2,1,0:T(8,128)S(1)} fusion(f32[9,1,64,128]{3,2,1,0:T(8,128)} %collective-permute-done.4, f32[9,1,64,128]{3,2,1,0:T(8,128)} %collective-permute-done.5, f32[8,4,64,128]{3,2,1,0:T(8,128)S(1)} %get-tuple-element.13, f32[1,4,64,128]{3,2,1,0:T(8,128)S(1)} %bitcast.54), kind=kLoop, calls=%fused_computation.10 | loop fusion | flops 8339760 | bytes 3622752 | tf_op jit(solution)/shard_map/concatenate | solution.py:19
  74.2 5.7 %fusion.44 = f32[9,4,64,128]{3,2,1,0:T(8,128)S(1)} fusion(f32[9,6,66,130]{3,2,1,0:T(8,128)S(1)} %select_maximum_fusion.3, f32[9,1,64,128]{3,2,1,0:T(8,128)} %collective-permute-done.5, f32[8,4,64,128]{3,2,1,0:T(8,128)S(1)} %get-tuple-element.13, f32[1,4,64,128]{3,2,1,0:T(8,128)S(1)} %bitcast.55, f32[9,1,64,128]{3,2,1,0:T(8,128)} %collective-permute-done.4, ...), kind=kLoop, calls=%fused_computation.87 | loop fusion | flops 20643840 | bytes 24182784 | tf_op jit(solution)/shard_map/add | solution.py:75
  80.0 0.1 fusion.97
  80.1 0.6 fusion.87
  80.6 0.0 copy-start.58
  80.7 0.9 fusion.91
  81.5 4.5 %collective-permute-start.7 = (f32[9,1,64,128]{3,2,1,0:T(8,128)}, f32[9,1,64,128]{3,2,1,0:T(8,128)}, u32[]{:S(2)}, u32[]{:S(2)}) collective-permute-start(f32[9,1,64,128]{3,2,1,0:T(8,128)} %get-tuple-element.21), channel_id=1, source_target_pairs={{0,2},{2,4},{4,6},{6,8},{8,10},{10,12},{12,14},{14,16},{16,18},{18... | collective-permute-start | bytes 884744 | tf_op jit(solution)/shard_map/ppermute | solution.py:15
  86.1 1.3 collective-permute-start.6
  87.4 0.5 compare_and_fusion.2
  87.9 8.6 %copy.14 = f32[8,4,64,128]{0,3,2,1:T(8,128)} copy(f32[8,4,64,128]{3,2,1,0:T(8,128)S(1)} %get-tuple-element.14) | data formatting | bytes 2097152 | tf_op jit(solution)/shard_map/add | solution.py:120
  96.6 7.0 %gather_fusion = f32[128,8]{1,0:T(8,128)} fusion(f32[8,32768]{0,1:T(8,128)} %bitcast.50, s32[1024]{0:T(1024)S(1)} %pad_clamp_fusion), kind=kCustom, calls=%fused_computation.clone | custom fusion | bytes 8704 | tf_op jit(solution)/shard_map/jit(_take)/gather | solution.py:121
  103.5 8.6 %copy.15 = f32[8,4,64,128]{0,3,2,1:T(8,128)} copy(f32[8,4,64,128]{3,2,1,0:T(8,128)S(1)} %get-tuple-element.12) | data formatting | bytes 2097152 | tf_op jit(solution)/shard_map/add | solution.py:120
  112.2 7.0 %gather_fusion.1 = f32[128,8]{1,0:T(8,128)} fusion(f32[8,32768]{0,1:T(8,128)} %bitcast.52, s32[1024]{0:T(1024)S(1)} %pad_clamp_fusion), kind=kCustom, calls=%fused_computation.1.clone | custom fusion | bytes 8704 | tf_op jit(solution)/shard_map/jit(_take)/gather | solution.py:121
  119.3 0.0 collective-permute-done.6
  119.3 3.9 %select_maximum_fusion = f32[9,6,66,130]{3,2,1,0:T(8,128)S(1)} fusion(f32[9,1,64,128]{3,2,1,0:T(8,128)} %collective-permute-done.6, f32[9,1,64,128]{3,2,1,0:T(8,128)} %collective-permute-done.7, f32[8,4,64,128]{3,2,1,0:T(8,128)S(1)} %get-tuple-element.11, f32[1,4,64,128]{3,2,1,0:T(8,128)S(1)} %bitcast.60), kind=kLoop, calls=%fused_computation.7 | loop fusion | flops 8339760 | bytes 3622752 | tf_op jit(solution)/shard_map/concatenate | solution.py:19
  123.4 5.7 %fusion.19 = f32[9,4,64,128]{3,2,1,0:T(8,128)S(1)} fusion(f32[9,6,66,130]{3,2,1,0:T(8,128)S(1)} %select_maximum_fusion, f32[9,1,64,128]{3,2,1,0:T(8,128)} %collective-permute-done.7, f32[8,4,64,128]{3,2,1,0:T(8,128)S(1)} %get-tuple-element.11, f32[1,4,64,128]{3,2,1,0:T(8,128)S(1)} %bitcast.61, f32[9,1,64,128]{3,2,1,0:T(8,128)} %collective-permute-done.6, ...), kind=kLoop, calls=%fused_computation.54 | loop fusion | flops 20643840 | bytes 24182784 | tf_op jit(solution)/shard_map/add | solution.py:75
  129.2 0.1 fusion.96
  129.3 0.4 fusion.84
  129.7 0.0 copy-start
  129.7 0.0 copy-start.53
  129.7 8.7 %copy.16 = f32[8,4,64,128]{0,3,2,1:T(8,128)} copy(f32[8,4,64,128]{3,2,1,0:T(8,128)S(1)} %fusion.84) | data formatting | bytes 2097152 | tf_op jit(solution)/shard_map/add | solution.py:120
  138.4 6.4 %gather_fusion.2 = f32[128,8]{1,0:T(8,128)S(1)} fusion(f32[8,32768]{0,1:T(8,128)} %bitcast.51, s32[1024]{0:T(1024)S(1)} %pad_clamp_fusion), kind=kCustom, calls=%fused_computation.2.clone | custom fusion | bytes 8704 | tf_op jit(solution)/shard_map/jit(_take)/gather | solution.py:121
  144.9 0.1 fusion.105
  145.0 78.4 %psum.7 = f32[8,128]{0,1:T(8,128)S(1)} all-reduce(f32[8,128]{0,1:T(8,128)S(1)} %fusion.105), channel_id=1, replica_groups=mesh['space'=16,'sens'=2] {'space'}, use_global_device_ids=true, to_apply=%region_3.5 | all-reduce | flops 1024 | bytes 8192 | tf_op jit(solution)/shard_map/psum | solution.py:124
  223.4 0.7 copy.17
  (127 shorter events, 0.3 us)
Async XLA Ops:
  0.6 10.5 %copy-start.52 = (s32[3]{0:T(128)S(1)}, s32[3]{0:T(128)}, u32[]{:S(2)}) copy-start(s32[3]{0:T(128)} %param.13) | copy-start | bytes 40
  0.6 19.0 %copy-start.60 = (f32[8,3]{0,1:T(4,128)S(1)}, f32[8,3]{0,1:T(4,128)}, u32[]{:S(2)}) copy-start(f32[8,3]{0,1:T(4,128)} %param.15) | copy-start | bytes 292
  0.7 19.0 %copy-start.49 = (f32[4,4,64,128]{3,2,1,0:T(8,128)S(1)}, f32[4,4,64,128]{3,2,1,0:T(8,128)}, u32[]{:S(2)}) copy-start(f32[4,4,64,128]{3,2,1,0:T(8,128)} %param.11) | copy-start | bytes 1572868
  4.2 18.2 %copy-start.62 = (s32[8]{0:T(128)S(1)}, s32[8]{0:T(128)}, u32[]{:S(2)}) copy-start(s32[8]{0:T(128)} %param.14) | copy-start | bytes 100
  4.2 18.2 %copy-start.1 = (f32[8,4,64,128]{3,2,1,0:T(8,128)S(1)}, f32[8,4,64,128]{3,2,1,0:T(8,128)}, u32[]{:S(2)}) copy-start(f32[8,4,64,128]{3,2,1,0:T(8,128)} %param.10) | copy-start | bytes 3145732
  4.2 28.6 %collective-permute-start = (f32[6,1,64,128]{3,2,1,0:T(8,128)}, f32[6,1,64,128]{3,2,1,0:T(8,128)}, u32[]{:S(2)}, u32[]{:S(2)}) collective-permute-start(f32[6,1,64,128]{3,2,1,0:T(8,128)} %get-tuple-element.27), channel_id=1, source_target_pairs={{0,2},{2,4},{4,6},{6,8},{8,10},{10,12},{12,14},{14,16},{16,18},{18... | collective-permute-start | bytes 589832 | tf_op jit(solution)/shard_map/ppermute | solution.py:15
  9.8 23.0 %collective-permute-start.1 = (f32[6,1,64,128]{3,2,1,0:T(8,128)}, f32[6,1,64,128]{3,2,1,0:T(8,128)}, u32[]{:S(2)}, u32[]{:S(2)}) collective-permute-start(f32[6,1,64,128]{3,2,1,0:T(8,128)} %get-tuple-element.28), channel_id=1, source_target_pairs={{2,0},{4,2},{6,4},{8,6},{10,8},{12,10},{14,12},{16,14},{18,16},{20... | collective-permute-start | bytes 589832 | tf_op jit(solution)/shard_map/ppermute | solution.py:18
  22.7 9.5 %copy-start.57 = (s32[128]{0:T(128)S(1)}, s32[128]{0:T(128)}, u32[]{:S(2)}) copy-start(s32[128]{0:T(128)} %param.17) | copy-start | bytes 1540
  22.7 9.5 %copy-start.61 = (s32[128]{0:T(128)S(1)}, s32[128]{0:T(128)}, u32[]{:S(2)}) copy-start(s32[128]{0:T(128)} %param.16) | copy-start | bytes 1540
  23.6 12.3 %collective-permute-start.3 = (f32[9,1,64,128]{3,2,1,0:T(8,128)}, f32[9,1,64,128]{3,2,1,0:T(8,128)}, u32[]{:S(2)}, u32[]{:S(2)}) collective-permute-start(f32[9,1,64,128]{3,2,1,0:T(8,128)} %get-tuple-element.25), channel_id=1, source_target_pairs={{0,2},{2,4},{4,6},{6,8},{8,10},{10,12},{12,14},{14,16},{16,18},{18... | collective-permute-start | bytes 884744 | tf_op jit(solution)/shard_map/ppermute | solution.py:15
  28.9 14.7 %collective-permute-start.2 = (f32[9,1,64,128]{3,2,1,0:T(8,128)}, f32[9,1,64,128]{3,2,1,0:T(8,128)}, u32[]{:S(2)}, u32[]{:S(2)}) collective-permute-start(f32[9,1,64,128]{3,2,1,0:T(8,128)} %get-tuple-element.26), channel_id=1, source_target_pairs={{2,0},{4,2},{6,4},{8,6},{10,8},{12,10},{14,12},{16,14},{18,16},{20... | collective-permute-start | bytes 884744 | tf_op jit(solution)/shard_map/ppermute | solution.py:18
  35.2 12.1 %copy-start.30 = (f32[4,64,128]{2,1,0:T(8,128)}, f32[4,64,128]{2,1,0:T(8,128)S(1)}, u32[]{:S(2)}) copy-start(f32[4,64,128]{2,1,0:T(8,128)S(1)} %get-tuple-element.38) | copy-start | bytes 393220
  35.2 12.1 %copy-start.33 = (f32[4,64,128]{2,1,0:T(8,128)}, f32[4,64,128]{2,1,0:T(8,128)S(1)}, u32[]{:S(2)}) copy-start(f32[4,64,128]{2,1,0:T(8,128)S(1)} %get-tuple-element.39) | copy-start | bytes 393220
  35.2 12.1 %copy-start.36 = (f32[4,64,128]{2,1,0:T(8,128)}, f32[4,64,128]{2,1,0:T(8,128)S(1)}, u32[]{:S(2)}) copy-start(f32[4,64,128]{2,1,0:T(8,128)S(1)} %get-tuple-element.40) | copy-start | bytes 393220
  35.2 12.1 %copy-start.39 = (f32[4,64,128]{2,1,0:T(8,128)}, f32[4,64,128]{2,1,0:T(8,128)S(1)}, u32[]{:S(2)}) copy-start(f32[4,64,128]{2,1,0:T(8,128)S(1)} %get-tuple-element.41) | copy-start | bytes 393220
  35.2 12.1 %copy-start.42 = (f32[4,64,128]{2,1,0:T(8,128)}, f32[4,64,128]{2,1,0:T(8,128)S(1)}, u32[]{:S(2)}) copy-start(f32[4,64,128]{2,1,0:T(8,128)S(1)} %get-tuple-element.64) | copy-start | bytes 393220
  35.3 12.1 %copy-start.45 = (f32[4,64,128]{2,1,0:T(8,128)}, f32[4,64,128]{2,1,0:T(8,128)S(1)}, u32[]{:S(2)}) copy-start(f32[4,64,128]{2,1,0:T(8,128)S(1)} %get-tuple-element.65) | copy-start | bytes 393220
  35.5 38.5 %copy-start.3 = (f32[4,64,128]{2,1,0:T(8,128)}, f32[4,64,128]{2,1,0:T(8,128)S(1)}, u32[]{:S(2)}) copy-start(f32[4,64,128]{2,1,0:T(8,128)S(1)} %get-tuple-element.35) | copy-start | bytes 393220
  35.6 38.5 %copy-start.5 = (f32[4,64,128]{2,1,0:T(8,128)}, f32[4,64,128]{2,1,0:T(8,128)S(1)}, u32[]{:S(2)}) copy-start(f32[4,64,128]{2,1,0:T(8,128)S(1)} %get-tuple-element.66) | copy-start | bytes 393220
  35.6 38.5 %copy-start.7 = (f32[4,64,128]{2,1,0:T(8,128)}, f32[4,64,128]{2,1,0:T(8,128)S(1)}, u32[]{:S(2)}) copy-start(f32[4,64,128]{2,1,0:T(8,128)S(1)} %get-tuple-element.67) | copy-start | bytes 393220
  35.9 11.5 %copy-start.15 = (f32[4,64,128]{2,1,0:T(8,128)}, f32[4,64,128]{2,1,0:T(8,128)S(1)}, u32[]{:S(2)}) copy-start(f32[4,64,128]{2,1,0:T(8,128)S(1)} %get-tuple-element.49) | copy-start | bytes 393220
  35.9 11.5 %copy-start.18 = (f32[4,64,128]{2,1,0:T(8,128)}, f32[4,64,128]{2,1,0:T(8,128)S(1)}, u32[]{:S(2)}) copy-start(f32[4,64,128]{2,1,0:T(8,128)S(1)} %get-tuple-element.60) | copy-start | bytes 393220
  35.9 11.5 %copy-start.21 = (f32[4,64,128]{2,1,0:T(8,128)}, f32[4,64,128]{2,1,0:T(8,128)S(1)}, u32[]{:S(2)}) copy-start(f32[4,64,128]{2,1,0:T(8,128)S(1)} %get-tuple-element.61) | copy-start | bytes 393220
  35.9 11.5 %copy-start.24 = (f32[4,64,128]{2,1,0:T(8,128)}, f32[4,64,128]{2,1,0:T(8,128)S(1)}, u32[]{:S(2)}) copy-start(f32[4,64,128]{2,1,0:T(8,128)S(1)} %get-tuple-element.62) | copy-start | bytes 393220
  35.9 11.5 %copy-start.27 = (f32[4,64,128]{2,1,0:T(8,128)}, f32[4,64,128]{2,1,0:T(8,128)S(1)}, u32[]{:S(2)}) copy-start(f32[4,64,128]{2,1,0:T(8,128)S(1)} %get-tuple-element.63) | copy-start | bytes 393220
  35.9 38.2 %copy-start.9 = (f32[4,64,128]{2,1,0:T(8,128)}, f32[4,64,128]{2,1,0:T(8,128)S(1)}, u32[]{:S(2)}) copy-start(f32[4,64,128]{2,1,0:T(8,128)S(1)} %get-tuple-element.46) | copy-start | bytes 393220
  35.9 38.2 %copy-start.11 = (f32[4,64,128]{2,1,0:T(8,128)}, f32[4,64,128]{2,1,0:T(8,128)S(1)}, u32[]{:S(2)}) copy-start(f32[4,64,128]{2,1,0:T(8,128)S(1)} %get-tuple-element.47) | copy-start | bytes 393220
  35.9 38.2 %copy-start.13 = (f32[4,64,128]{2,1,0:T(8,128)}, f32[4,64,128]{2,1,0:T(8,128)S(1)}, u32[]{:S(2)}) copy-start(f32[4,64,128]{2,1,0:T(8,128)S(1)} %get-tuple-element.48) | copy-start | bytes 393220
  47.4 5.9 %copy-start.2 = (f32[8,4,64,128]{3,2,1,0:T(8,128)S(1)}, f32[8,4,64,128]{3,2,1,0:T(8,128)}, u32[]{:S(2)}) copy-start(f32[8,4,64,128]{3,2,1,0:T(8,128)} %param.10) | copy-start | bytes 3145732
  53.8 5.4 %copy-start.48 = (f32[1,4,64,128]{3,2,1,0:T(8,128)S(1)}, f32[1,4,64,128]{3,2,1,0:T(8,128)}, u32[]{:S(2)}) copy-start(f32[1,4,64,128]{3,2,1,0:T(8,128)} %get-tuple-element.30) | copy-start | bytes 393220
  54.7 14.9 %collective-permute-start.5 = (f32[9,1,64,128]{3,2,1,0:T(8,128)}, f32[9,1,64,128]{3,2,1,0:T(8,128)}, u32[]{:S(2)}, u32[]{:S(2)}) collective-permute-start(f32[9,1,64,128]{3,2,1,0:T(8,128)} %get-tuple-element.23), channel_id=1, source_target_pairs={{0,2},{2,4},{4,6},{6,8},{8,10},{10,12},{12,14},{14,16},{16,18},{18... | collective-permute-start | bytes 884744 | tf_op jit(solution)/shard_map/ppermute | solution.py:15
  57.9 12.4 %collective-permute-start.4 = (f32[9,1,64,128]{3,2,1,0:T(8,128)}, f32[9,1,64,128]{3,2,1,0:T(8,128)}, u32[]{:S(2)}, u32[]{:S(2)}) collective-permute-start(f32[9,1,64,128]{3,2,1,0:T(8,128)} %get-tuple-element.24), channel_id=1, source_target_pairs={{2,0},{4,2},{6,4},{8,6},{10,8},{12,10},{14,12},{16,14},{18,16},{20... | collective-permute-start | bytes 884744 | tf_op jit(solution)/shard_map/ppermute | solution.py:18
  62.6 11.5 %copy-start.16 = (f32[4,64,128]{2,1,0:T(8,128)S(1)}, f32[4,64,128]{2,1,0:T(8,128)}, u32[]{:S(2)}) copy-start(f32[4,64,128]{2,1,0:T(8,128)} %copy-done.15) | copy-start | bytes 393220
  62.6 11.5 %copy-start.19 = (f32[4,64,128]{2,1,0:T(8,128)S(1)}, f32[4,64,128]{2,1,0:T(8,128)}, u32[]{:S(2)}) copy-start(f32[4,64,128]{2,1,0:T(8,128)} %copy-done.18) | copy-start | bytes 393220
  62.6 11.5 %copy-start.22 = (f32[4,64,128]{2,1,0:T(8,128)S(1)}, f32[4,64,128]{2,1,0:T(8,128)}, u32[]{:S(2)}) copy-start(f32[4,64,128]{2,1,0:T(8,128)} %copy-done.21) | copy-start | bytes 393220
  62.6 11.5 %copy-start.25 = (f32[4,64,128]{2,1,0:T(8,128)S(1)}, f32[4,64,128]{2,1,0:T(8,128)}, u32[]{:S(2)}) copy-start(f32[4,64,128]{2,1,0:T(8,128)} %copy-done.24) | copy-start | bytes 393220
  62.6 11.5 %copy-start.28 = (f32[4,64,128]{2,1,0:T(8,128)S(1)}, f32[4,64,128]{2,1,0:T(8,128)}, u32[]{:S(2)}) copy-start(f32[4,64,128]{2,1,0:T(8,128)} %copy-done.27) | copy-start | bytes 393220
  62.7 11.5 %copy-start.31 = (f32[4,64,128]{2,1,0:T(8,128)S(1)}, f32[4,64,128]{2,1,0:T(8,128)}, u32[]{:S(2)}) copy-start(f32[4,64,128]{2,1,0:T(8,128)} %copy-done.30) | copy-start | bytes 393220
  62.7 11.5 %copy-start.34 = (f32[4,64,128]{2,1,0:T(8,128)S(1)}, f32[4,64,128]{2,1,0:T(8,128)}, u32[]{:S(2)}) copy-start(f32[4,64,128]{2,1,0:T(8,128)} %copy-done.33) | copy-start | bytes 393220
  62.7 11.5 %copy-start.37 = (f32[4,64,128]{2,1,0:T(8,128)S(1)}, f32[4,64,128]{2,1,0:T(8,128)}, u32[]{:S(2)}) copy-start(f32[4,64,128]{2,1,0:T(8,128)} %copy-done.36) | copy-start | bytes 393220
  62.7 11.5 %copy-start.40 = (f32[4,64,128]{2,1,0:T(8,128)S(1)}, f32[4,64,128]{2,1,0:T(8,128)}, u32[]{:S(2)}) copy-start(f32[4,64,128]{2,1,0:T(8,128)} %copy-done.39) | copy-start | bytes 393220
  62.7 11.5 %copy-start.43 = (f32[4,64,128]{2,1,0:T(8,128)S(1)}, f32[4,64,128]{2,1,0:T(8,128)}, u32[]{:S(2)}) copy-start(f32[4,64,128]{2,1,0:T(8,128)} %copy-done.42) | copy-start | bytes 393220
  62.7 11.5 %copy-start.46 = (f32[4,64,128]{2,1,0:T(8,128)S(1)}, f32[4,64,128]{2,1,0:T(8,128)}, u32[]{:S(2)}) copy-start(f32[4,64,128]{2,1,0:T(8,128)} %copy-done.45) | copy-start | bytes 393220
  80.6 6.7 %copy-start.56 = (s32[128]{0:T(128)S(1)}, s32[128]{0:T(128)}, u32[]{:S(2)}) copy-start(s32[128]{0:T(128)} %get-tuple-element.56) | copy-start | bytes 1540
  80.6 6.7 %copy-start.58 = (s32[128]{0:T(128)S(1)}, s32[128]{0:T(128)}, u32[]{:S(2)}) copy-start(s32[128]{0:T(128)} %param.17) | copy-start | bytes 1540
  80.7 6.7 %copy-start.59 = (pred[128]{0:T(512)(128)(4,1)S(1)}, pred[128]{0:T(512)(128)(4,1)}, u32[]{:S(2)}) copy-start(pred[128]{0:T(512)(128)(4,1)} %get-tuple-element.8) | copy-start | bytes 388
  81.5 37.8 %collective-permute-start.7 = (f32[9,1,64,128]{3,2,1,0:T(8,128)}, f32[9,1,64,128]{3,2,1,0:T(8,128)}, u32[]{:S(2)}, u32[]{:S(2)}) collective-permute-start(f32[9,1,64,128]{3,2,1,0:T(8,128)} %get-tuple-element.21), channel_id=1, source_target_pairs={{0,2},{2,4},{4,6},{6,8},{8,10},{10,12},{12,14},{14,16},{16,18},{18... | collective-permute-start | bytes 884744 | tf_op jit(solution)/shard_map/ppermute | solution.py:15
  86.1 33.3 %collective-permute-start.6 = (f32[9,1,64,128]{3,2,1,0:T(8,128)}, f32[9,1,64,128]{3,2,1,0:T(8,128)}, u32[]{:S(2)}, u32[]{:S(2)}) collective-permute-start(f32[9,1,64,128]{3,2,1,0:T(8,128)} %get-tuple-element.22), channel_id=1, source_target_pairs={{2,0},{4,2},{6,4},{8,6},{10,8},{12,10},{14,12},{16,14},{18,16},{20... | collective-permute-start | bytes 884744 | tf_op jit(solution)/shard_map/ppermute | solution.py:18
  119.2 4.1 %copy-start.12 = (f32[4,64,128]{2,1,0:T(8,128)S(1)}, f32[4,64,128]{2,1,0:T(8,128)}, u32[]{:S(2)}) copy-start(f32[4,64,128]{2,1,0:T(8,128)} %copy-done.11) | copy-start | bytes 393220
  119.2 4.1 %copy-start.14 = (f32[4,64,128]{2,1,0:T(8,128)S(1)}, f32[4,64,128]{2,1,0:T(8,128)}, u32[]{:S(2)}) copy-start(f32[4,64,128]{2,1,0:T(8,128)} %copy-done.13) | copy-start | bytes 393220
  119.2 4.1 %copy-start.17 = (f32[4,64,128]{2,1,0:T(8,128)S(1)}, f32[4,64,128]{2,1,0:T(8,128)}, u32[]{:S(2)}) copy-start(f32[4,64,128]{2,1,0:T(8,128)} %copy-done.15) | copy-start | bytes 393220
  119.2 4.1 %copy-start.20 = (f32[4,64,128]{2,1,0:T(8,128)S(1)}, f32[4,64,128]{2,1,0:T(8,128)}, u32[]{:S(2)}) copy-start(f32[4,64,128]{2,1,0:T(8,128)} %copy-done.18) | copy-start | bytes 393220
  119.2 4.1 %copy-start.23 = (f32[4,64,128]{2,1,0:T(8,128)S(1)}, f32[4,64,128]{2,1,0:T(8,128)}, u32[]{:S(2)}) copy-start(f32[4,64,128]{2,1,0:T(8,128)} %copy-done.21) | copy-start | bytes 393220
  119.2 4.1 %copy-start.26 = (f32[4,64,128]{2,1,0:T(8,128)S(1)}, f32[4,64,128]{2,1,0:T(8,128)}, u32[]{:S(2)}) copy-start(f32[4,64,128]{2,1,0:T(8,128)} %copy-done.24) | copy-start | bytes 393220
  119.3 4.1 %copy-start.29 = (f32[4,64,128]{2,1,0:T(8,128)S(1)}, f32[4,64,128]{2,1,0:T(8,128)}, u32[]{:S(2)}) copy-start(f32[4,64,128]{2,1,0:T(8,128)} %copy-done.27) | copy-start | bytes 393220
  119.3 4.1 %copy-start.32 = (f32[4,64,128]{2,1,0:T(8,128)S(1)}, f32[4,64,128]{2,1,0:T(8,128)}, u32[]{:S(2)}) copy-start(f32[4,64,128]{2,1,0:T(8,128)} %copy-done.30) | copy-start | bytes 393220
  119.3 4.1 %copy-start.35 = (f32[4,64,128]{2,1,0:T(8,128)S(1)}, f32[4,64,128]{2,1,0:T(8,128)}, u32[]{:S(2)}) copy-start(f32[4,64,128]{2,1,0:T(8,128)} %copy-done.33) | copy-start | bytes 393220
  119.3 4.1 %copy-start.38 = (f32[4,64,128]{2,1,0:T(8,128)S(1)}, f32[4,64,128]{2,1,0:T(8,128)}, u32[]{:S(2)}) copy-start(f32[4,64,128]{2,1,0:T(8,128)} %copy-done.36) | copy-start | bytes 393220
  129.7 8.8 %copy-start = (f32[8,4,64,128]{3,2,1,0:T(8,128)}, f32[8,4,64,128]{3,2,1,0:T(8,128)S(1)}, u32[]{:S(2)}) copy-start(f32[8,4,64,128]{3,2,1,0:T(8,128)S(1)} %fusion.84) | copy-start | bytes 3145732
  129.7 15.2 %copy-start.50 = (f32[128,8]{1,0:T(8,128)S(1)}, f32[128,8]{1,0:T(8,128)}, u32[]{:S(2)}) copy-start(f32[128,8]{1,0:T(8,128)} %gather_fusion) | copy-start | bytes 12292
  129.7 15.2 %copy-start.51 = (f32[128,8]{1,0:T(8,128)S(1)}, f32[128,8]{1,0:T(8,128)}, u32[]{:S(2)}) copy-start(f32[128,8]{1,0:T(8,128)} %gather_fusion.1) | copy-start | bytes 12292
  129.7 15.2 %copy-start.53 = (pred[128]{0:T(512)(128)(4,1)S(1)}, pred[128]{0:T(512)(128)(4,1)}, u32[]{:S(2)}) copy-start(pred[128]{0:T(512)(128)(4,1)} %get-tuple-element.7) | copy-start | bytes 388
  129.7 15.2 %copy-start.54 = (pred[128]{0:T(512)(128)(4,1)S(1)}, pred[128]{0:T(512)(128)(4,1)}, u32[]{:S(2)}) copy-start(pred[128]{0:T(512)(128)(4,1)} %get-tuple-element.55) | copy-start | bytes 388
  129.7 15.2 %copy-start.55 = (pred[128]{0:T(512)(128)(4,1)S(1)}, pred[128]{0:T(512)(128)(4,1)}, u32[]{:S(2)}) copy-start(pred[128]{0:T(512)(128)(4,1)} %get-tuple-element.54) | copy-start | bytes 388
  (7 other events, 28.7 us)
